TPU v7x, 512 devices: a whole 4x8x8 slice. The times are simulated.
512 devices in a mesh: member: 16 (over y_hi, z), tile: 32 (over x, y_lo, core).
Axes of the slice: x: 4, y: 8 (y_hi: 2, y_lo: 4; y = y_hi * 4 + y_lo), z: 8, core: 2. Of those that a mesh axis runs over, the one named last changes fastest.
Arguments:
- anomalies: bfloat16 [16, 256, 2, 128, 128], P('member', 'tile'), may hold values from -6 to 6
- weights: bfloat16 [16, 256, 16], P('member', 'tile'), may hold values from -2 to 2
- diffusivity: float32 [256, 128, 128], P('tile'), may hold values from 0.05 to 1.2
- land_mask: int32 [256, 128, 128], P('tile'), may hold values 0 or 1
- neighbours: int32 [256, 4], P('tile'), may hold values from -1 to 255, as said below
Outputs:
- analysis_increment: bfloat16 [16, 256, 2, 128, 128], P('member', 'tile')
Inputs may be any that keep to these rules, and one draw needn't show every extreme that they name: Tile t is held by tile device t // 8. Its west and east neighbours always exist and are tiles of the previous and next tile device, wrapping around; its south and north neighbours are tiles of the same device or -1. The relation is symmetric (west against east, south against north).
All inputs are finite; a program needn't handle non-finite values. No bound on the sum of `land_mask` on one device may be relied on, other than what follows from the above.
Results may differ from a plain program's by a relative error of at most 0.0015.
Values may be sent and summed in bfloat16 or wider, within the bound.
A program may use at most 64 MiB of HBM per device.

v0:
```python
import jax
import jax.numpy as jnp
from jax import lax
from jax.sharding import PartitionSpec as P

PASSES = 4


diffusion_rate = 0.2


def extended_2(cells, sides, width):
    for axis, dim in sides:
        count = lax.axis_size(axis)
        head = lax.slice_in_dim(cells, 0, width, axis=dim)
        tail = lax.slice_in_dim(cells, cells.shape[dim] - width, cells.shape[dim], axis=dim)
        cells = jnp.concatenate(
            [
                lax.ppermute(tail, axis, [(i, (i + 1) % count) for i in range(count)]),
                cells,
                lax.ppermute(head, axis, [((i + 1) % count, i) for i in range(count)]),
            ],
            axis=dim,
        )
    return cells


def select_rows(targets, first_index, table):
    row_count = table.shape[1]
    chooser = (
        targets[:, None] == first_index + jnp.arange(row_count, dtype=jnp.int32)[None, :]
    ).astype(jnp.float32)
    return jnp.einsum("sr,arcx->ascx", chooser, table, precision=lax.Precision.HIGHEST)


def assemble(tracer_field, west_edge, east_edge, south_edge, north_edge):
    middle = jnp.concatenate([west_edge[..., None], tracer_field, east_edge[..., None]], axis=-1)
    spread = [(0, 0)] * (south_edge.ndim - 1) + [(1, 1)]
    south_edge = jnp.pad(south_edge, spread)
    north_edge = jnp.pad(north_edge, spread)
    return jnp.concatenate([south_edge[..., None, :], middle, north_edge[..., None, :]], axis=-2)


def extend(tracer_field, neighbours):
    slot_count = tracer_field.shape[1]
    tile_devices = lax.axis_size("tile")
    position = lax.axis_index("tile")
    own_first = position * slot_count
    before = jnp.mod(position - 1, tile_devices) * slot_count
    next_first = jnp.mod(position + 1, tile_devices) * slot_count
    west_cols = tracer_field[..., :, 0]
    east_cols = tracer_field[..., :, -1]
    col_shape = west_cols.shape
    face_cols = jnp.stack([west_cols.reshape(-1), east_cols.reshape(-1)], 0)
    extended = extended_2(face_cols, (("tile", 0),), 1)
    from_west = extended[0].reshape(col_shape)
    from_east = extended[3].reshape(col_shape)
    west_edge = select_rows(neighbours[:, 0], before, from_west)
    east_edge = select_rows(neighbours[:, 1], next_first, from_east)
    south_edge = select_rows(neighbours[:, 2], own_first, tracer_field[..., -1, :])
    north_edge = select_rows(neighbours[:, 3], own_first, tracer_field[..., 0, :])
    return assemble(tracer_field, west_edge, east_edge, south_edge, north_edge)


def face_weights(padded):
    centre = padded[..., 1:-1, 1:-1]
    return (
        jnp.sqrt(centre * padded[..., 1:-1, 2:]),
        jnp.sqrt(centre * padded[..., 1:-1, :-2]),
        jnp.sqrt(centre * padded[..., 2:, 1:-1]),
        jnp.sqrt(centre * padded[..., :-2, 1:-1]),
    )


def shards(anomalies, weights, diffusivity, land_mask, neighbours):
    summed = lax.psum_scatter(
        jnp.einsum("ktcij,ktm->mtcij", anomalies, weights, preferred_element_type=jnp.float32),
        "member",
        scatter_dimension=0,
        tiled=True,
    )
    wet_cells = land_mask.astype(jnp.float32)
    increment = summed * wet_cells[None, :, None]
    coefficient = (diffusivity * wet_cells)[None, :, None]
    east_w, west_w, north_w, south_w = face_weights(extend(coefficient, neighbours))
    for sweep_index in range(PASSES):
        padded = extend(increment, neighbours)
        change = east_w * (padded[..., 1:-1, 2:] - increment) + west_w * (
            padded[..., 1:-1, :-2] - increment
        )
        change = (
            change
            + north_w * (padded[..., 2:, 1:-1] - increment)
            + south_w * (padded[..., :-2, 1:-1] - increment)
        )
        increment = increment + diffusion_rate * change
    return increment.astype(jnp.bfloat16)


def solution(mesh):
    return jax.shard_map(
        shards,
        mesh=mesh,
        in_specs=(
            P("member", "tile", None, None, None),
            P("member", "tile", None),
            P("tile", None, None),
            P("tile", None, None),
            P("tile", None),
        ),
        out_specs=P("member", "tile", None, None, None),
        check_vma=False,
    )
```

profile of v0, /device:TPU:6, one launch (start us, length us, event | category | flops | bytes accessed | tf_op | source)
XLA Modules:
  0.0 544.9 jit_solution(9435542273556431450)
XLA Ops:
  6.5 1.1 bitcast_convert_fusion
  7.7 0.6 copy.75
  8.3 0.7 bitcast_convert_fusion.1
  9.1 7.4 %multiply_bitcast_fusion = f32[16,8,2,128,128]{4,1,2,3,0:T(8,128)} fusion(f32[8,2,128,128]{3,0,1,2:T(8,128)S(1)} %copy.75, f32[8,16]{0,1:T(8,128)S(1)} %copy.74), kind=kLoop, calls=%fused_computation | loop fusion | flops 4194304 | bytes 17826304 | tf_op jit(solution)/shard_map/ktcij,ktm->mtcij/transpose | solution.py:77
  17.1 5.2 collective-permute-start
  22.3 1.9 collective-permute-start.2
  25.5 1.0 copy.77
  27.5 2.4 collective-permute-done.2
  30.1 1.7 fusion.58
  32.1 1.5 copy.89
  33.6 2.2 copy.83
  35.8 2.2 copy.79
  38.0 420.2 %reduce-scatter.2.cloned.1.call-done = f32[1,8,2,128,128]{4,1,2,3,0:T(8,128)} async-done(((f32[16,8,2,128,128]{4,1,2,3,0:T(8,128)}), f32[1,8,2,128,128]{4,1,2,3,0:T(8,128)}) %reduce-scatter.2.cloned.1.call-update) | async-done | bytes 1048592 | tf_op jit(solution)/shard_map/reduce_scatter | solution.py:76
  458.2 1.5 broadcast_multiply_fusion
  460.1 1.4 fusion.90
  461.4 1.6 copy.80
  463.1 1.9 collective-permute-start.1
  465.0 0.5 copy.84
  465.4 2.4 collective-permute-start.3
  468.1 1.5 copy.82
  469.6 3.5 collective-permute-done.3
  473.3 1.4 copy.86
  474.7 4.0 fusion.44
  478.9 1.4 fusion.89
  480.5 1.6 copy.95
  482.1 2.3 collective-permute-start.4
  484.9 2.2 collective-permute-start.5
  487.4 0.5 copy.97
  487.9 4.7 collective-permute-done.5
  492.8 1.5 copy.100
  494.2 4.0 fusion.31
  498.5 1.4 fusion.88
  500.1 1.6 copy.103
  501.7 1.9 collective-permute-start.6
  504.1 2.4 collective-permute-start.7
  506.8 1.5 copy.105
  508.2 3.5 collective-permute-done.7
  512.0 1.4 copy.108
  513.4 4.4 fusion.18
  517.9 1.4 fusion.87
  519.5 1.6 copy.111
  521.2 2.3 collective-permute-start.8
  523.9 2.0 collective-permute-start.9
  526.2 0.5 copy.113
  526.7 4.9 collective-permute-done.9
  531.8 1.5 copy.116
  533.3 3.8 fusion.5
  537.1 0.9 copy.119
  (69 shorter events, 8.1 us)
Async XLA Ops:
  6.5 451.7 %reduce-scatter.2.cloned.1.call-start = ((), (), s32[]{:S(2)}) async-start(), calls=%async_computation.1 | async-start | bytes 17825792 | tf_op jit(solution)/shard_map/reduce_scatter | solution.py:76
  9.1 7.4 %copy-start.4 = (s32[8,128,128]{2,1,0:T(8,128)S(1)}, s32[8,128,128]{2,1,0:T(8,128)}, u32[]{:S(2)}) copy-start(s32[8,128,128]{2,1,0:T(8,128)} %param.8) | copy-start | bytes 1572868
  9.1 7.7 %copy-start.5 = (f32[8,128,128]{2,1,0:T(8,128)S(1)}, f32[8,128,128]{2,1,0:T(8,128)}, u32[]{:S(2)}) copy-start(f32[8,128,128]{2,1,0:T(8,128)} %param.7) | copy-start | bytes 1572868
  9.1 15.8 %copy-start.6 = (s32[8,4]{0,1:T(4,128)S(1)}, s32[8,4]{0,1:T(4,128)}, u32[]{:S(2)}) copy-start(s32[8,4]{0,1:T(4,128)} %param.9) | copy-start | bytes 388
  17.1 10.3 %collective-permute-start = (f32[1,1024]{1,0:T(1,128)S(1)}, f32[1,1024]{1,0:T(1,128)S(1)}, u32[]{:S(2)}, u32[]{:S(2)}) collective-permute-start(f32[1,1024]{1,0:T(1,128)S(1)} %bitcast.231), channel_id=1, source_target_pairs={{1,0},{2,1},{3,2},{4,3},{5,4},{6,5},{7,6},{8,7},{9,8},{10,9},{11,1... | collective-permute-start | bytes 12296 | tf_op jit(solution)/shard_map/ppermute | solution.py:21
  22.3 7.6 %collective-permute-start.2 = (f32[1,1024]{1,0:T(1,128)S(1)}, f32[1,1024]{1,0:T(1,128)S(1)}, u32[]{:S(2)}, u32[]{:S(2)}) collective-permute-start(f32[1,1024]{1,0:T(1,128)S(1)} %bitcast.230), channel_id=1, source_target_pairs={{0,1},{1,2},{2,3},{3,4},{4,5},{5,6},{6,7},{7,8},{8,9},{9,10},{10,1... | collective-permute-start | bytes 12296 | tf_op jit(solution)/shard_map/ppermute | solution.py:19
  32.1 460.7 %copy-start = (f32[8,128,128]{2,0,1:T(8,128)}, f32[8,128,128]{2,0,1:T(8,128)S(1)}, u32[]{:S(2)}) copy-start(f32[8,128,128]{2,0,1:T(8,128)S(1)} %copy.94) | copy-start | bytes 1572868
  33.6 459.2 %copy-start.2 = (f32[8,128,128]{2,0,1:T(8,128)}, f32[8,128,128]{2,0,1:T(8,128)S(1)}, u32[]{:S(2)}) copy-start(f32[8,128,128]{2,0,1:T(8,128)S(1)} %copy.89) | copy-start | bytes 1572868
  463.1 4.9 collective-permute-start.1
  465.4 7.7 %collective-permute-start.3 = (f32[1,2048]{1,0:T(1,128)S(1)}, f32[1,2048]{1,0:T(1,128)S(1)}, u32[]{:S(2)}, u32[]{:S(2)}) collective-permute-start(f32[1,2048]{1,0:T(1,128)S(1)} %bitcast.222), channel_id=1, source_target_pairs={{0,1},{1,2},{2,3},{3,4},{4,5},{5,6},{6,7},{7,8},{8,9},{9,10},{10,1... | collective-permute-start | bytes 24584 | tf_op jit(solution)/shard_map/ppermute | solution.py:19
  482.1 5.0 collective-permute-start.4
  484.9 7.7 %collective-permute-start.5 = (f32[1,2048]{1,0:T(1,128)S(1)}, f32[1,2048]{1,0:T(1,128)S(1)}, u32[]{:S(2)}, u32[]{:S(2)}) collective-permute-start(f32[1,2048]{1,0:T(1,128)S(1)} %bitcast.225), channel_id=1, source_target_pairs={{0,1},{1,2},{2,3},{3,4},{4,5},{5,6},{6,7},{7,8},{8,9},{9,10},{10,1... | collective-permute-start | bytes 24584 | tf_op jit(solution)/shard_map/ppermute | solution.py:19
  498.3 35.0 %copy-start.1 = (f32[8,128,128]{2,0,1:T(8,128)S(1)}, f32[8,128,128]{2,0,1:T(8,128)}, u32[]{:S(2)}) copy-start(f32[8,128,128]{2,0,1:T(8,128)} %copy-done) | copy-start | bytes 1572868
  498.3 35.0 %copy-start.3 = (f32[8,128,128]{2,0,1:T(8,128)S(1)}, f32[8,128,128]{2,0,1:T(8,128)}, u32[]{:S(2)}) copy-start(f32[8,128,128]{2,0,1:T(8,128)} %copy-done.2) | copy-start | bytes 1572868
  501.7 4.8 collective-permute-start.6
  504.1 7.7 %collective-permute-start.7 = (f32[1,2048]{1,0:T(1,128)S(1)}, f32[1,2048]{1,0:T(1,128)S(1)}, u32[]{:S(2)}, u32[]{:S(2)}) collective-permute-start(f32[1,2048]{1,0:T(1,128)S(1)} %bitcast.226), channel_id=1, source_target_pairs={{0,1},{1,2},{2,3},{3,4},{4,5},{5,6},{6,7},{7,8},{8,9},{9,10},{10,1... | collective-permute-start | bytes 24584 | tf_op jit(solution)/shard_map/ppermute | solution.py:19
  521.2 4.8 collective-permute-start.8
  523.9 7.7 %collective-permute-start.9 = (f32[1,2048]{1,0:T(1,128)S(1)}, f32[1,2048]{1,0:T(1,128)S(1)}, u32[]{:S(2)}, u32[]{:S(2)}) collective-permute-start(f32[1,2048]{1,0:T(1,128)S(1)} %bitcast.224), channel_id=1, source_target_pairs={{0,1},{1,2},{2,3},{3,4},{4,5},{5,6},{6,7},{7,8},{8,9},{9,10},{10,1... | collective-permute-start | bytes 24584 | tf_op jit(solution)/shard_map/ppermute | solution.py:19
Sparse Core Ops, SparseCore 0:
  16.6 441.5 reduce-scatter.1
where the time goes:
time: 550 us; the launch traced here: 545 us
  waiting for transfers between devices  439 us (80%)
  local copies, waits for them, and re-layouts  34.9 us (6%)
  other arithmetic  28.7 us (5%)
  starting transfers between devices  24.5 us (4%)
  between operations  13.8 us (3%)
    reduce_scatter x1, waiting for transfers between devices, shards(): lax.psum_scatter(jnp.einsum('ktcij,ktm->mtcij', anomalies, weights, prefe...  420 us
    ppermute x5, waiting for transfers between devices, extended_2(): lax.ppermute(tail, axis, [(i, (i + 1) % count) for i in range(count)])  18.9 us
    ppermute x5, starting transfers between devices, extended_2(): lax.ppermute(head, axis, [((i + 1) % count, i) for i in range(count)])  13.7 us
    add x3, other arithmetic, shards(): increment = increment + diffusion_rate * change  12.4 us
  transfers between devices with their start and end apart: 11, of which 6 were waited for; matrix products, arithmetic and copies ran while one was open for 3% of the time, Pallas kernels for 0%

commit v1 on v0

v1 whole, which is shorter than its diff:
```python
import functools

import jax
import jax.numpy as jnp
from jax import lax
from jax.experimental import pallas as pl
from jax.experimental.pallas import tpu as pltpu
from jax.sharding import PartitionSpec as P

MESH = pl.DeviceIdType.MESH
F32 = jnp.float32

RATE = 0.2
SLOTS = 8
N = 128
TRACERS = 2
UNITS = TRACERS * SLOTS
RAW = 3
SUMMED = UNITS - RAW
TRAVEL = UNITS + RAW
RING = 8
LAG = 2
Y_LAG = 6
LAST = 4 * LAG
STEPS = max(TRAVEL + LAST, SUMMED + LAST + Y_LAG)
TOP = 16
PAD = 160
ZERO = SLOTS


def kernel(
    anomalies,
    weights,
    diffusivity,
    land_mask,
    neighbours,
    out,
    blocks,
    own_w,
    splat,
    own_sum,
    away_sum,
    here_sum,
    first,
    second,
    root,
    keep,
    gain,
    inverse,
    diff_in,
    mask_in,
    strips_0,
    strips_1,
    strips_root,
    tables,
    links,
    z_send,
    z_recv,
    w_send,
    w_recv,
    y_send,
    y_recv,
    s_send,
    s_recv,
    t_send,
    t_recv,
    load,
):
    member = lax.axis_index("member")
    tile = lax.axis_index("tile")
    strips = (strips_0, strips_1, strips_root)
    half, z = member // RING, lax.rem(member, RING)
    partner = lax.rem(member + RING, 2 * RING)
    up = (half * RING + lax.rem(z + 1, RING), tile)
    down = (half * RING + lax.rem(z + RING - 1, RING), tile)
    across = (partner, tile)
    tile_devices = lax.axis_size("tile")
    before = lax.rem(tile + tile_devices - 1, tile_devices)
    behind = lax.rem(tile + 1, tile_devices)
    west, east = (member, before), (member, behind)

    def remote(src, dst, send, recv, device):
        return pltpu.make_async_remote_copy(
            src_ref=src,
            dst_ref=dst,
            send_sem=send,
            recv_sem=recv,
            device_id=device,
            device_id_type=MESH,
        )

    loads = [
        pltpu.make_async_copy(
            anomalies.at[:, c], blocks.at[0, pl.ds(c * SLOTS, SLOTS)], load.at[c]
        )
        for c in range(TRACERS)
    ]
    loads.append(pltpu.make_async_copy(diffusivity, diff_in, load.at[TRACERS]))
    loads.append(pltpu.make_async_copy(land_mask, mask_in, load.at[TRACERS + 1]))
    for copy in loads:
        copy.start()

    barrier = pltpu.get_barrier_semaphore()
    for device in (up, down, across, west, east):
        pl.semaphore_signal(barrier, inc=1, device_id=device, device_id_type=MESH)

    spread = (
        lax.broadcasted_iota(jnp.int32, (16, N), 0)
        == lax.broadcasted_iota(jnp.int32, (16, N), 1)
    ).astype(jnp.bfloat16)
    padded = jnp.dot(weights[...], spread, preferred_element_type=F32)
    own_w[0, 0] = jnp.concatenate([padded, jnp.zeros_like(padded)], axis=0).astype(
        jnp.bfloat16
    )
    pl.semaphore_wait(barrier, 5)

    def ring(v, slot):
        rightward = slot < RING // 2
        return remote(
            blocks.at[slot - 1 if rightward else (slot + 1) % RING, v],
            blocks.at[slot, v],
            z_send.at[v * RING + slot],
            z_recv.at[v * RING + slot],
            up if rightward else down,
        )

    def ring_far_right(v):
        return remote(
            blocks.at[3, v], blocks.at[4, v], z_send.at[v * RING + 4], z_recv.at[v * RING + 4], up
        )

    def ring_far_left(v):
        return remote(
            blocks.at[5, v], blocks.at[4, v], z_send.at[v * RING + 4], z_recv.at[v * RING + 4], down
        )

    def ring_w(g, slot):
        rightward = slot <= RING // 2
        return remote(
            own_w.at[g, slot - 1 if rightward else (slot + 1) % RING],
            own_w.at[g, slot],
            w_send.at[g * RING + slot],
            w_recv.at[g * RING + slot],
            up if rightward else down,
        )

    def cross_raw(k):
        return remote(
            anomalies.at[SUMMED + k - SLOTS, 1], blocks.at[0, UNITS + k], y_send.at[UNITS + k], y_recv.at[UNITS + k], across
        )

    def cross_w():
        return remote(own_w.at[0, 0], own_w.at[1, 0], w_send.at[RING], w_recv.at[RING], across)

    def cross_sum(u):
        return remote(away_sum.at[u], here_sum.at[u], y_send.at[u], y_recv.at[u], across)

    def strip_copies(field, c):
        return (
            remote(
                field.at[pl.ds(0, SLOTS), pl.ds(TOP, 8)], strips[c].at[1], s_send.at[c * 2], s_recv.at[c * 2], west
            ),
            remote(
                field.at[pl.ds(0, SLOTS), pl.ds(TOP + N - 8, 8)],
                strips[c].at[0],
                s_send.at[c * 2 + 1],
                s_recv.at[c * 2 + 1],
                east,
            ),
        )

    def table_copies():
        return (
            remote(neighbours, tables.at[1], t_send.at[0], t_recv.at[0], west),
            remote(neighbours, tables.at[0], t_send.at[1], t_recv.at[1], east),
        )

    def send_own(s):
        ring(s, 1).start()
        ring(s, RING - 1).start()

    def send_first(v):
        for slot, device in ((1, up), (RING - 1, down)):
            remote(
                anomalies.at[v, 0], blocks.at[slot, v], z_send.at[v * RING + slot], z_recv.at[v * RING + slot], device
            ).start()

    send_first(0)
    ring_w(0, 1).start()
    ring_w(0, RING - 1).start()
    send_first(1)
    cross_w().start()
    for k in range(RAW):
        cross_raw(k).start()
    for copy in table_copies():
        copy.start()
    for copy in loads:
        copy.wait()

    root[ZERO] = jnp.zeros((PAD, N), F32)
    for field in (first, second):
        for c in range(TRACERS):
            field[c, ZERO] = jnp.zeros((PAD, N), F32)

    @pl.loop(0, SLOTS)
    def _(t):
        coefficient = diff_in[t] * mask_in[t].astype(F32)
        side = jnp.sqrt(RATE * coefficient).T
        root[t, pl.ds(TOP, N)] = side
        wet = side > 0
        inverse[t] = jnp.where(wet, 1.0 / jnp.where(wet, side, 1.0), 0.0)

    for copy in strip_copies(root, TRACERS):
        copy.start()

    lane = lax.broadcasted_iota(jnp.int32, (8, N), 1)

    def set_splat(g, row, owner):
        for s in range(RING):
            w = own_w[g, s].astype(F32)[:SLOTS]
            chosen = jnp.sum(jnp.where(lane == owner, w, 0.0), axis=1, keepdims=True)
            splat[row, s] = jnp.broadcast_to(chosen, (SLOTS, N))

    def sum_unit(u):
        t = lax.rem(u, SLOTS)
        mine = [splat[0, s, pl.ds(t, 1)] for s in range(RING)]
        theirs = [splat[1, s, pl.ds(t, 1)] for s in range(RING)]

        @pl.loop(0, N // 16)
        def _(i):
            rows = pl.ds(pl.multiple_of(i * 16, 16), 16)
            for s in range(RING):
                x = blocks[s, u, rows].astype(F32)
                if s == 0:
                    a, b = x * mine[s], x * theirs[s]
                else:
                    a, b = a + x * mine[s], b + x * theirs[s]
            own_sum[u, rows] = a
            away_sum[u, rows] = b

    def sum_raw(k):
        u = SUMMED + k
        t = lax.rem(u, SLOTS)
        mine = [splat[0, s, pl.ds(t, 1)] for s in range(RING)]
        theirs = [splat[2, s, pl.ds(t, 1)] for s in range(RING)]

        @pl.loop(0, N // 16)
        def _(i):
            rows = pl.ds(pl.multiple_of(i * 16, 16), 16)
            for s in range(RING):
                x, y = blocks[s, u, rows].astype(F32), blocks[s, UNITS + k, rows].astype(F32)
                if s == 0:
                    a = x * mine[s] + y * theirs[s]
                else:
                    a = a + (x * mine[s] + y * theirs[s])
            own_sum[u, rows] = a

    def place(u, total):
        c, t = u // SLOTS, lax.rem(u, SLOTS)
        first[c, t, pl.ds(TOP, N)] = total.T * root[t, pl.ds(TOP, N)]

    def unpack(field, c):
        @pl.loop(0, SLOTS)
        def _(t):
            field[t, pl.ds(TOP - 8, 8)] = strips[c][0, links[t, 0]]
            field[t, pl.ds(TOP + N, 8)] = strips[c][1, links[t, 1]]

    def read_tables():
        for copy in table_copies():
            copy.wait()
        def local(index):
            return jnp.where(index < 0, ZERO, lax.rem(jnp.maximum(index, 0), SLOTS))

        @pl.loop(0, SLOTS)
        def _(t):
            w, e = (lax.rem(jnp.maximum(neighbours[t, k], 0), SLOTS) for k in (0, 1))
            links[t, 0] = w
            links[t, 1] = e
            for k in (2, 3):
                links[t, k] = local(neighbours[t, k])
                for side, slot, back, at in ((0, w, 1, 2), (1, e, 0, 4)):
                    beyond = tables[side, slot, k]
                    via = tables[side, lax.rem(jnp.maximum(beyond, 0), SLOTS), back]
                    links[t, at + k] = jnp.where(beyond < 0, ZERO, local(via))

    lane16 = lax.broadcasted_iota(jnp.int32, (16, N), 1)

    def around(field, t, r, size, south, north):
        lanes = lane16[:size]
        y = field[t, pl.ds(r, size)]
        to_north = pltpu.roll(jnp.where(lanes == 0, field[north, pl.ds(r, size)], y), N - 1, 1)
        to_south = pltpu.roll(jnp.where(lanes == N - 1, field[south, pl.ds(r, size)], y), 1, 1)
        return (field[t, pl.ds(r + 1, size)] + field[t, pl.ds(r - 1, size)]) + (to_north + to_south)

    def pieces(t, with_strips):
        if with_strips:
            yield TOP - 8, 8, links[t, 4], links[t, 5]
        for r in range(TOP, TOP + N, 16):
            yield r, 16, links[t, 2], links[t, 3]
        if with_strips:
            yield TOP + N, 8, links[t, 6], links[t, 7]

    def set_gains():
        for copy in strip_copies(root, TRACERS):
            copy.wait()
        read_tables()
        unpack(root, TRACERS)

        @pl.loop(0, SLOTS)
        def _(t):
            for r, size, south, north in pieces(t, True):
                side = root[t, pl.ds(r, size)]
                keep[t, pl.ds(r, size)] = 1.0 - side * around(root, t, r, size, south, north)
                gain[t, pl.ds(r, size)] = side * side

    def sweep(source, target, c, with_strips):
        here, there = source.at[c], target.at[c]

        @pl.loop(0, SLOTS)
        def _(t):
            for r, size, south, north in pieces(t, with_strips):
                rows = pl.ds(r, size)
                there[t, rows] = keep[t, rows] * here[t, rows] + gain[t, rows] * around(
                    here, t, r, size, south, north
                )

    def begin(c):
        for copy in strip_copies(first.at[c], c):
            copy.start()

    def arrived(c):
        for copy in strip_copies(first.at[c], c):
            copy.wait()
        unpack(first.at[c], c)

    def finish(c):
        here = first.at[c]

        @pl.loop(0, SLOTS)
        def _(t):
            rows = pl.ds(TOP, N)
            out[t, c] = (here[t, rows] * inverse[t]).T.astype(jnp.bfloat16)

    def step(s):
        for d in (3, 2, 1):
            v = s - LAG * d

            @pl.when(jnp.logical_and(v >= 0, v < TRAVEL))
            def _():
                ring(v, d).wait_recv()
                if d < 3:
                    ring(v, d + 1).start()
                else:

                    @pl.when(lax.rem(v, 2) == 0)
                    def _():
                        ring_far_right(v).start()

                ring(v, RING - d).wait_recv()
                if d < 3:
                    ring(v, RING - d - 1).start()
                else:

                    @pl.when(lax.rem(v, 2) == 1)
                    def _():
                        ring_far_left(v).start()

            for g, at in ((0, 0), (1, UNITS)):

                @pl.when(v == at)
                def _():
                    ring_w(g, d).wait_recv()
                    ring_w(g, d + 1).start()
                    ring_w(g, RING - d).wait_recv()
                    if d < 3:
                        ring_w(g, RING - d - 1).start()

        @pl.when(s == UNITS)
        def _():
            cross_w().wait_recv()
            ring_w(1, 1).start()
            ring_w(1, RING - 1).start()

        @pl.when(jnp.logical_and(s >= UNITS, s < TRAVEL))
        def _():
            cross_raw(s - UNITS).wait_recv()

        @pl.when(s < TRAVEL)
        def _():
            send_own(s)

        v = s - LAST

        @pl.when(v == 0)
        def _():
            ring_w(0, 4).wait_recv()
            set_splat(0, 0, member)
            set_splat(0, 1, partner)

        @pl.when(v == UNITS)
        def _():
            ring_w(1, 4).wait_recv()
            set_splat(1, 2, member)

        @pl.when(jnp.logical_and(v >= 0, v < TRAVEL))
        def _():
            ring_far_right(v).wait_recv()

        @pl.when(jnp.logical_and(v >= 0, v < SUMMED))
        def _():
            sum_unit(v)
            cross_sum(v).start()

        @pl.when(jnp.logical_and(v >= UNITS, v < TRAVEL))
        def _():
            k = v - UNITS
            sum_raw(k)
            place(SUMMED + k, own_sum[SUMMED + k])

        u = v - Y_LAG

        @pl.when(jnp.logical_and(u >= 0, u < SUMMED))
        def _():
            cross_sum(u).wait_recv()
            place(u, own_sum[u] + here_sum[u])

        @pl.when(s == LAST + 2)
        def _():
            set_gains()

        @pl.when(u == SLOTS - 1)
        def _():
            begin(0)

    pl.loop(2, STEPS)(step)

    begin(1)

    arrived(0)
    sweep(first, second, 0, True)
    sweep(second, first, 0, True)
    sweep(first, second, 0, True)
    sweep(second, first, 0, False)
    finish(0)

    @pl.loop(0, TRAVEL)
    def _(v):
        for slot in (1, 2, 3, 5, 6, 7):
            ring(v, slot).wait_send()
        ring_far_right(v).wait_send()

    for g in range(2):
        for slot in range(1, RING):
            ring_w(g, slot).wait_send()
    cross_w().wait_send()

    @pl.loop(0, SUMMED)
    def _(u):
        cross_sum(u).wait_send()

    for k in range(RAW):
        cross_raw(k).wait_send()

    arrived(1)
    sweep(first, second, 1, True)
    sweep(second, first, 1, True)
    sweep(first, second, 1, True)
    sweep(second, first, 1, False)
    finish(1)


def shards(anomalies, weights, diffusivity, land_mask, neighbours):
    anywhere = pl.BlockSpec(memory_space=pl.ANY)
    vmem = pl.BlockSpec(memory_space=pltpu.VMEM)
    smem = pl.BlockSpec(memory_space=pltpu.SMEM)
    result = pl.pallas_call(
        kernel,
        out_shape=jax.ShapeDtypeStruct((SLOTS, TRACERS, N, N), jnp.bfloat16),
        in_specs=[anywhere, vmem, anywhere, anywhere, smem],
        out_specs=vmem,
        scratch_shapes=[
            pltpu.VMEM((RING, TRAVEL, N, N), jnp.bfloat16),
            pltpu.VMEM((2, RING, 16, N), jnp.bfloat16),
            pltpu.VMEM((3, RING, SLOTS, N), F32),
            pltpu.VMEM((UNITS, N, N), F32),
            pltpu.VMEM((SUMMED, N, N), F32),
            pltpu.VMEM((SUMMED, N, N), F32),
            pltpu.VMEM((TRACERS, SLOTS + 1, PAD, N), F32),
            pltpu.VMEM((TRACERS, SLOTS + 1, PAD, N), F32),
            pltpu.VMEM((SLOTS + 1, PAD, N), F32),
            pltpu.VMEM((SLOTS, PAD, N), F32),
            pltpu.VMEM((SLOTS, PAD, N), F32),
            pltpu.VMEM((SLOTS, N, N), F32),
            pltpu.VMEM((SLOTS, N, N), F32),
            pltpu.VMEM((SLOTS, N, N), jnp.int32),
            pltpu.VMEM((2, SLOTS, 8, N), F32),
            pltpu.VMEM((2, SLOTS, 8, N), F32),
            pltpu.VMEM((2, SLOTS, 8, N), F32),
            pltpu.SMEM((2, SLOTS, 4), jnp.int32),
            pltpu.SMEM((SLOTS, 8), jnp.int32),
            pltpu.SemaphoreType.DMA((TRAVEL * RING,)),
            pltpu.SemaphoreType.DMA((TRAVEL * RING,)),
            pltpu.SemaphoreType.DMA((2 * RING,)),
            pltpu.SemaphoreType.DMA((2 * RING,)),
            pltpu.SemaphoreType.DMA((TRAVEL,)),
            pltpu.SemaphoreType.DMA((TRAVEL,)),
            pltpu.SemaphoreType.DMA((2 * TRACERS + 2,)),
            pltpu.SemaphoreType.DMA((2 * TRACERS + 2,)),
            pltpu.SemaphoreType.DMA((2,)),
            pltpu.SemaphoreType.DMA((2,)),
            pltpu.SemaphoreType.DMA((TRACERS + 2,)),
        ],
        compiler_params=pltpu.CompilerParams(
            collective_id=0, has_side_effects=True, vmem_limit_bytes=48 << 20
        ),
    )(anomalies[0], weights[0], diffusivity, land_mask, neighbours)
    return result[None]


def solution(mesh):
    return jax.shard_map(
        shards,
        mesh=mesh,
        in_specs=(
            P("member", "tile", None, None, None),
            P("member", "tile", None),
            P("tile", None, None),
            P("tile", None, None),
            P("tile", None),
        ),
        out_specs=P("member", "tile", None, None, None),
        check_vma=False,
    )
```

time: 550 us -> 88.6 us (0.16)
  waiting for transfers between devices: 439 us -> 0 us
  Pallas kernels: 0 us -> 83 us
  local copies, waits for them, and re-layouts: 34.9 us -> 5.28 us
  other arithmetic: 28.7 us -> 0 us
  starting transfers between devices: 24.5 us -> 0 us
  between operations: 13.8 us -> 0.01 us
    reduce_scatter x1 -> x0, waiting for transfers between devices: 420 us -> none  [shards(): lax.psum_scatter(jnp.einsum('ktcij,ktm->mtcij', anomalies, weights, prefe...]
    pallas_call x0 -> x1, Pallas kernels: none -> 83 us  [shards(): pl.pallas_call(kernel, out_shape=jax.ShapeDtypeStruct((SLOTS, TRACERS, N,...]
    ppermute x10 -> x0, starting transfers between devices: 24.5 us -> none  [the longest x5 13.7 us: extended_2(): lax.ppermute(head, axis, [((i + 1) % count, i) for i in range(count)])]
    ppermute x10 -> x0, waiting for transfers between devices: 19 us -> none  [the longest x5 18.9 us: extended_2(): lax.ppermute(tail, axis, [(i, (i + 1) % count) for i in range(count)])]
    slice x16 -> x0, local copies, waits for them, and re-layouts: 14.4 us -> none  [the longest x9 7.24 us: extend(): east_cols = tracer_field[..., :, -1]]
    add x6 -> x0, other arithmetic: 12.4 us -> none  [the longest x3 12.4 us: shards(): increment = increment + diffusion_rate * change]
    broadcast_in_dim x19 -> x0, local copies, waits for them, and re-layouts: 11.2 us -> none  [the longest x4 5.74 us: assemble(): west_edge[..., None]]
    transpose x1 -> x0, other arithmetic: 7.39 us -> none  [shards(): jnp.einsum('ktcij,ktm->mtcij', anomalies, weights, preferred_element_type...]
  transfers between devices with their start and end apart: 11 -> 0, of which waited for: 6 -> 0; matrix products, arithmetic and copies ran while one was open for 3% -> 0% of each run, Pallas kernels for 0% -> 0%
where the time goes in v1:
time: 88.6 us; the launch traced here: 88.3 us
  Pallas kernels  83 us (94%)
  local copies, waits for them, and re-layouts  5.28 us (6%)
    pallas_call x1, Pallas kernels, shards(): pl.pallas_call(kernel, out_shape=jax.ShapeDtypeStruct((SLOTS, TRACERS, N,...  83 us
    unnamed x12, local copies, waits for them, and re-layouts  5.28 us

profile of v1, /device:TPU:6, one launch (start us, length us, event | category | flops | bytes accessed | tf_op | source)
XLA Modules:
  0.0 88.3 jit_solution(4825349056077486987)
XLA Ops:
  0.0 0.0 copy-start.4
  0.0 0.7 copy-done.4
  0.7 0.0 copy-start.3
  0.7 0.1 copy.6.neighbours
  0.8 0.6 copy-done.3
  1.4 0.0 copy-start
  1.4 1.0 %copy-done = bf16[1,8,2,128,128]{4,3,2,1,0:T(8,128)(2,1)S(1)} copy-done((bf16[1,8,2,128,128]{4,3,2,1,0:T(8,128)(2,1)S(1)}, bf16[1,8,2,128,128]{4,3,2,1,0:T(8,128)(2,1)}, u32[]{:S(2)}) %copy-start) | copy-done | bytes 524312
  2.4 0.0 copy-start.1
  2.4 1.0 %copy-done.1 = f32[8,128,128]{2,1,0:T(8,128)S(1)} copy-done((f32[8,128,128]{2,1,0:T(8,128)S(1)}, f32[8,128,128]{2,1,0:T(8,128)}, u32[]{:S(2)}) %copy-start.1) | copy-done | bytes 524312
  3.4 0.0 copy-start.2
  3.5 1.0 %copy-done.2 = s32[8,128,128]{2,1,0:T(8,128)S(1)} copy-done((s32[8,128,128]{2,1,0:T(8,128)S(1)}, s32[8,128,128]{2,1,0:T(8,128)}, u32[]{:S(2)}) %copy-start.2) | copy-done | bytes 524312
  4.5 83.0 %shard_map.55 = bf16[8,2,128,128]{3,2,1,0:T(8,128)(2,1)S(1)} custom-call(bf16[8,2,128,128]{3,2,1,0:T(8,128)(2,1)S(1)} %bitcast.4, bf16[8,16]{1,0:T(8,128)(2,1)S(1)} %bitcast.5, f32[8,128,128]{2,1,0:T(8,128)S(1)} %copy-done.1, s32[8,128,128]{2,1,0:T(8,128)S(1)} %copy-done.2, s32[8,4]{1,0:T(8,128)S(1)} %copy.6.neighbours), custom_call_target="tpu_custom_call" | custom-call | tf_op jit(solution)/shard_map/pallas_call | solution.py:476
  87.5 0.8 copy.8
Async XLA Ops:
  0.0 0.7 copy-start.4
  0.7 0.7 copy-start.3
  1.4 1.0 %copy-start = (bf16[1,8,2,128,128]{4,3,2,1,0:T(8,128)(2,1)S(1)}, bf16[1,8,2,128,128]{4,3,2,1,0:T(8,128)(2,1)}, u32[]{:S(2)}) copy-start(bf16[1,8,2,128,128]{4,3,2,1,0:T(8,128)(2,1)} %param.5) | copy-start | bytes 1572868
  2.4 1.0 %copy-start.1 = (f32[8,128,128]{2,1,0:T(8,128)S(1)}, f32[8,128,128]{2,1,0:T(8,128)}, u32[]{:S(2)}) copy-start(f32[8,128,128]{2,1,0:T(8,128)} %diffusivity.1) | copy-start | bytes 1572868
  3.4 1.0 %copy-start.2 = (s32[8,128,128]{2,1,0:T(8,128)S(1)}, s32[8,128,128]{2,1,0:T(8,128)}, u32[]{:S(2)}) copy-start(s32[8,128,128]{2,1,0:T(8,128)} %land_mask.1) | copy-start | bytes 1572868

commit v2 on v1

--- a/solution.py
+++ b/solution.py
@@ -33,7 +33,7 @@
     weights,
     diffusivity,
     land_mask,
-    neighbours,
+    neighbour_table,
     out,
     blocks,
     own_w,
@@ -54,6 +54,8 @@
     strips_root,
     tables,
     links,
+    neighbours,
+    weights_in,
     z_send,
     z_recv,
     w_send,
@@ -89,29 +91,24 @@
             device_id_type=MESH,
         )
 
-    loads = [
-        pltpu.make_async_copy(
-            anomalies.at[:, c], blocks.at[0, pl.ds(c * SLOTS, SLOTS)], load.at[c]
-        )
-        for c in range(TRACERS)
-    ]
-    loads.append(pltpu.make_async_copy(diffusivity, diff_in, load.at[TRACERS]))
-    loads.append(pltpu.make_async_copy(land_mask, mask_in, load.at[TRACERS + 1]))
-    for copy in loads:
-        copy.start()
-
     barrier = pltpu.get_barrier_semaphore()
     for device in (up, down, across, west, east):
         pl.semaphore_signal(barrier, inc=1, device_id=device, device_id_type=MESH)
 
-    spread = (
-        lax.broadcasted_iota(jnp.int32, (16, N), 0)
-        == lax.broadcasted_iota(jnp.int32, (16, N), 1)
-    ).astype(jnp.bfloat16)
-    padded = jnp.dot(weights[...], spread, preferred_element_type=F32)
-    own_w[0, 0] = jnp.concatenate([padded, jnp.zeros_like(padded)], axis=0).astype(
-        jnp.bfloat16
-    )
+    loads = [
+        pltpu.make_async_copy(weights, weights_in, load.at[0]),
+        pltpu.make_async_copy(neighbour_table, neighbours, load.at[1]),
+        pltpu.make_async_copy(diffusivity, diff_in, load.at[2]),
+        pltpu.make_async_copy(land_mask, mask_in, load.at[3]),
+    ]
+    for c in range(TRACERS):
+        loads.append(
+            pltpu.make_async_copy(
+                anomalies.at[:, c], blocks.at[0, pl.ds(c * SLOTS, SLOTS)], load.at[4 + c]
+            )
+        )
+    for copy in loads:
+        copy.start()
     pl.semaphore_wait(barrier, 5)
 
     def ring(v, slot):
@@ -186,15 +183,26 @@
             ).start()
 
     send_first(0)
+    send_first(1)
+    for k in range(RAW):
+        cross_raw(k).start()
+
+    loads[0].wait()
+    spread = (
+        lax.broadcasted_iota(jnp.int32, (16, N), 0)
+        == lax.broadcasted_iota(jnp.int32, (16, N), 1)
+    ).astype(jnp.bfloat16)
+    padded = jnp.dot(weights_in[...], spread, preferred_element_type=F32)
+    own_w[0, 0] = jnp.concatenate([padded, jnp.zeros_like(padded)], axis=0).astype(
+        jnp.bfloat16
+    )
     ring_w(0, 1).start()
     ring_w(0, RING - 1).start()
-    send_first(1)
     cross_w().start()
-    for k in range(RAW):
-        cross_raw(k).start()
+    loads[1].wait()
     for copy in table_copies():
         copy.start()
-    for copy in loads:
+    for copy in loads[2:]:
         copy.wait()
 
     root[ZERO] = jnp.zeros((PAD, N), F32)
@@ -300,29 +308,35 @@
         if with_strips:
             yield TOP + N, 8, links[t, 6], links[t, 7]
 
-    def set_gains():
+    def prepare_gains():
         for copy in strip_copies(root, TRACERS):
             copy.wait()
         read_tables()
         unpack(root, TRACERS)
 
-        @pl.loop(0, SLOTS)
-        def _(t):
-            for r, size, south, north in pieces(t, True):
-                side = root[t, pl.ds(r, size)]
-                keep[t, pl.ds(r, size)] = 1.0 - side * around(root, t, r, size, south, north)
-                gain[t, pl.ds(r, size)] = side * side
+    def set_gains(t):
+        results = []
+        for r, size, south, north in pieces(t, True):
+            side = root[t, pl.ds(r, size)]
+            results.append((r, size, 1.0 - side * around(root, t, r, size, south, north), side * side))
+        for r, size, kept, gained in results:
+            keep[t, pl.ds(r, size)] = kept
+            gain[t, pl.ds(r, size)] = gained
 
     def sweep(source, target, c, with_strips):
         here, there = source.at[c], target.at[c]
 
-        @pl.loop(0, SLOTS)
+        @pl.loop(0, SLOTS, unroll=2)
         def _(t):
+            results = []
             for r, size, south, north in pieces(t, with_strips):
                 rows = pl.ds(r, size)
-                there[t, rows] = keep[t, rows] * here[t, rows] + gain[t, rows] * around(
+                value = keep[t, rows] * here[t, rows] + gain[t, rows] * around(
                     here, t, r, size, south, north
                 )
+                results.append((rows, value))
+            for rows, value in results:
+                there[t, rows] = value
 
     def begin(c):
         for copy in strip_copies(first.at[c], c):
@@ -336,7 +350,7 @@
     def finish(c):
         here = first.at[c]
 
-        @pl.loop(0, SLOTS)
+        @pl.loop(0, SLOTS, unroll=4)
         def _(t):
             rows = pl.ds(TOP, N)
             out[t, c] = (here[t, rows] * inverse[t]).T.astype(jnp.bfloat16)
@@ -424,9 +438,13 @@
             cross_sum(u).wait_recv()
             place(u, own_sum[u] + here_sum[u])
 
-        @pl.when(s == LAST + 2)
-        def _():
-            set_gains()
+        @pl.when(s == LAST + 1)
+        def _():
+            prepare_gains()
+
+        @pl.when(jnp.logical_and(s >= LAST + 2, s < LAST + 2 + SLOTS))
+        def _():
+            set_gains(s - (LAST + 2))
 
         @pl.when(u == SLOTS - 1)
         def _():
@@ -472,11 +490,10 @@
 def shards(anomalies, weights, diffusivity, land_mask, neighbours):
     anywhere = pl.BlockSpec(memory_space=pl.ANY)
     vmem = pl.BlockSpec(memory_space=pltpu.VMEM)
-    smem = pl.BlockSpec(memory_space=pltpu.SMEM)
     result = pl.pallas_call(
         kernel,
         out_shape=jax.ShapeDtypeStruct((SLOTS, TRACERS, N, N), jnp.bfloat16),
-        in_specs=[anywhere, vmem, anywhere, anywhere, smem],
+        in_specs=[anywhere] * 5,
         out_specs=vmem,
         scratch_shapes=[
             pltpu.VMEM((RING, TRAVEL, N, N), jnp.bfloat16),
@@ -498,6 +515,8 @@
             pltpu.VMEM((2, SLOTS, 8, N), F32),
             pltpu.SMEM((2, SLOTS, 4), jnp.int32),
             pltpu.SMEM((SLOTS, 8), jnp.int32),
+            pltpu.SMEM((SLOTS, 4), jnp.int32),
+            pltpu.VMEM((SLOTS, 16), jnp.bfloat16),
             pltpu.SemaphoreType.DMA((TRAVEL * RING,)),
             pltpu.SemaphoreType.DMA((TRAVEL * RING,)),
             pltpu.SemaphoreType.DMA((2 * RING,)),
@@ -508,7 +527,7 @@
             pltpu.SemaphoreType.DMA((2 * TRACERS + 2,)),
             pltpu.SemaphoreType.DMA((2,)),
             pltpu.SemaphoreType.DMA((2,)),
-            pltpu.SemaphoreType.DMA((TRACERS + 2,)),
+            pltpu.SemaphoreType.DMA((TRACERS + 4,)),
         ],
         compiler_params=pltpu.CompilerParams(
             collective_id=0, has_side_effects=True, vmem_limit_bytes=48 << 20

time: 88.6 us -> 84.8 us (0.957)
  Pallas kernels: 83 us -> 78.5 us
    pallas_call x1, Pallas kernels: 83 us -> 78.5 us  [shards(): pl.pallas_call(kernel, out_shape=jax.ShapeDtypeStruct((SLOTS, TRACERS, N,...]
where the time goes in v2:
time: 84.8 us; the launch traced here: 83.8 us
  Pallas kernels  78.5 us (93%)
  local copies, waits for them, and re-layouts  5.28 us (6%)
    pallas_call x1, Pallas kernels, shards(): pl.pallas_call(kernel, out_shape=jax.ShapeDtypeStruct((SLOTS, TRACERS, N,...  78.5 us
    unnamed x12, local copies, waits for them, and re-layouts  5.28 us

profile of v2, /device:TPU:6, one launch (start us, length us, event | category | flops | bytes accessed | tf_op | source)
XLA Modules:
  0.0 83.8 jit_solution(3762909986235909003)
XLA Ops:
  0.0 0.0 copy-start.4
  0.0 0.7 copy-done.4
  0.7 0.0 copy-start.3
  0.7 0.1 copy.6.neighbour_table
  0.8 0.6 copy-done.3
  1.4 0.0 copy-start
  1.4 1.0 %copy-done = bf16[1,8,2,128,128]{4,3,2,1,0:T(8,128)(2,1)S(1)} copy-done((bf16[1,8,2,128,128]{4,3,2,1,0:T(8,128)(2,1)S(1)}, bf16[1,8,2,128,128]{4,3,2,1,0:T(8,128)(2,1)}, u32[]{:S(2)}) %copy-start) | copy-done | bytes 524312
  2.4 0.0 copy-start.1
  2.4 1.0 %copy-done.1 = f32[8,128,128]{2,1,0:T(8,128)S(1)} copy-done((f32[8,128,128]{2,1,0:T(8,128)S(1)}, f32[8,128,128]{2,1,0:T(8,128)}, u32[]{:S(2)}) %copy-start.1) | copy-done | bytes 524312
  3.4 0.0 copy-start.2
  3.5 1.0 %copy-done.2 = s32[8,128,128]{2,1,0:T(8,128)S(1)} copy-done((s32[8,128,128]{2,1,0:T(8,128)S(1)}, s32[8,128,128]{2,1,0:T(8,128)}, u32[]{:S(2)}) %copy-start.2) | copy-done | bytes 524312
  4.5 78.5 %shard_map.55 = bf16[8,2,128,128]{3,2,1,0:T(8,128)(2,1)S(1)} custom-call(bf16[8,2,128,128]{3,2,1,0:T(8,128)(2,1)S(1)} %bitcast.4, bf16[8,16]{1,0:T(8,128)(2,1)S(1)} %bitcast.5, f32[8,128,128]{2,1,0:T(8,128)S(1)} %copy-done.1, s32[8,128,128]{2,1,0:T(8,128)S(1)} %copy-done.2, s32[8,4]{1,0:T(8,128)S(1)} %copy.6.neighbour_table), custom_call_target="tpu_custom_call" | custom-call | tf_op jit(solution)/shard_map/pallas_call | solution.py:493
  83.0 0.8 copy.8
Async XLA Ops:
  0.0 0.7 copy-start.4
  0.7 0.7 copy-start.3
  1.4 1.0 %copy-start = (bf16[1,8,2,128,128]{4,3,2,1,0:T(8,128)(2,1)S(1)}, bf16[1,8,2,128,128]{4,3,2,1,0:T(8,128)(2,1)}, u32[]{:S(2)}) copy-start(bf16[1,8,2,128,128]{4,3,2,1,0:T(8,128)(2,1)} %param.5) | copy-start | bytes 1572868
  2.4 1.0 %copy-start.1 = (f32[8,128,128]{2,1,0:T(8,128)S(1)}, f32[8,128,128]{2,1,0:T(8,128)}, u32[]{:S(2)}) copy-start(f32[8,128,128]{2,1,0:T(8,128)} %diffusivity.1) | copy-start | bytes 1572868
  3.4 1.0 %copy-start.2 = (s32[8,128,128]{2,1,0:T(8,128)S(1)}, s32[8,128,128]{2,1,0:T(8,128)}, u32[]{:S(2)}) copy-start(s32[8,128,128]{2,1,0:T(8,128)} %land_mask.1) | copy-start | bytes 1572868

commit v3 on v2

--- a/solution.py
+++ b/solution.py
@@ -19,9 +19,9 @@
 SUMMED = UNITS - RAW
 TRAVEL = UNITS + RAW
 RING = 8
-LAG = 2
+LAGS = (4, 7, 9, 10)
 Y_LAG = 6
-LAST = 4 * LAG
+LAST = LAGS[3]
 STEPS = max(TRAVEL + LAST, SUMMED + LAST + Y_LAG)
 TOP = 16
 PAD = 160
@@ -300,12 +300,14 @@
         to_south = pltpu.roll(jnp.where(lanes == N - 1, field[south, pl.ds(r, size)], y), 1, 1)
         return (field[t, pl.ds(r + 1, size)] + field[t, pl.ds(r - 1, size)]) + (to_north + to_south)
 
-    def pieces(t, with_strips):
-        if with_strips:
+    def pieces(t, with_strips, part=None):
+        inner = range(TOP + 16, TOP + N - 16, 16)
+        if with_strips and part != 0:
             yield TOP - 8, 8, links[t, 4], links[t, 5]
         for r in range(TOP, TOP + N, 16):
-            yield r, 16, links[t, 2], links[t, 3]
-        if with_strips:
+            if part is None or (r in inner) == (part == 0):
+                yield r, 16, links[t, 2], links[t, 3]
+        if with_strips and part != 0:
             yield TOP + N, 8, links[t, 6], links[t, 7]
 
     def prepare_gains():
@@ -323,13 +325,13 @@
             keep[t, pl.ds(r, size)] = kept
             gain[t, pl.ds(r, size)] = gained
 
-    def sweep(source, target, c, with_strips):
+    def sweep(source, target, c, with_strips, part=None):
         here, there = source.at[c], target.at[c]
 
         @pl.loop(0, SLOTS, unroll=2)
         def _(t):
             results = []
-            for r, size, south, north in pieces(t, with_strips):
+            for r, size, south, north in pieces(t, with_strips, part):
                 rows = pl.ds(r, size)
                 value = keep[t, rows] * here[t, rows] + gain[t, rows] * around(
                     here, t, r, size, south, north
@@ -357,7 +359,7 @@
 
     def step(s):
         for d in (3, 2, 1):
-            v = s - LAG * d
+            v = s - LAGS[d - 1]
 
             @pl.when(jnp.logical_and(v >= 0, v < TRAVEL))
             def _():
@@ -479,8 +481,9 @@
     for k in range(RAW):
         cross_raw(k).wait_send()
 
+    sweep(first, second, 1, True, 0)
     arrived(1)
-    sweep(first, second, 1, True)
+    sweep(first, second, 1, True, 1)
     sweep(second, first, 1, True)
     sweep(first, second, 1, True)
     sweep(second, first, 1, False)

time: 84.8 us -> 85 us (level)
  Pallas kernels: 78.5 us -> 79.4 us
    pallas_call x1, Pallas kernels: 78.5 us -> 79.4 us  [shards(): pl.pallas_call(kernel, out_shape=jax.ShapeDtypeStruct((SLOTS, TRACERS, N,...]
where the time goes in v3:
time: 85 us; the launch traced here: 84.7 us
  Pallas kernels  79.4 us (93%)
  local copies, waits for them, and re-layouts  5.28 us (6%)
    pallas_call x1, Pallas kernels, shards(): pl.pallas_call(kernel, out_shape=jax.ShapeDtypeStruct((SLOTS, TRACERS, N,...  79.4 us
    unnamed x12, local copies, waits for them, and re-layouts  5.28 us

profile of v3, /device:TPU:6, one launch (start us, length us, event | category | flops | bytes accessed | tf_op | source)
XLA Modules:
  0.0 84.7 jit_solution(2718524244729646319)
XLA Ops:
  0.0 0.0 copy-start.4
  0.0 0.7 copy-done.4
  0.7 0.0 copy-start.3
  0.7 0.1 copy.6.neighbour_table
  0.8 0.6 copy-done.3
  1.4 0.0 copy-start
  1.4 1.0 %copy-done = bf16[1,8,2,128,128]{4,3,2,1,0:T(8,128)(2,1)S(1)} copy-done((bf16[1,8,2,128,128]{4,3,2,1,0:T(8,128)(2,1)S(1)}, bf16[1,8,2,128,128]{4,3,2,1,0:T(8,128)(2,1)}, u32[]{:S(2)}) %copy-start) | copy-done | bytes 524312
  2.4 0.0 copy-start.1
  2.4 1.0 %copy-done.1 = f32[8,128,128]{2,1,0:T(8,128)S(1)} copy-done((f32[8,128,128]{2,1,0:T(8,128)S(1)}, f32[8,128,128]{2,1,0:T(8,128)}, u32[]{:S(2)}) %copy-start.1) | copy-done | bytes 524312
  3.4 0.0 copy-start.2
  3.5 1.0 %copy-done.2 = s32[8,128,128]{2,1,0:T(8,128)S(1)} copy-done((s32[8,128,128]{2,1,0:T(8,128)S(1)}, s32[8,128,128]{2,1,0:T(8,128)}, u32[]{:S(2)}) %copy-start.2) | copy-done | bytes 524312
  4.5 79.4 %shard_map.55 = bf16[8,2,128,128]{3,2,1,0:T(8,128)(2,1)S(1)} custom-call(bf16[8,2,128,128]{3,2,1,0:T(8,128)(2,1)S(1)} %bitcast.4, bf16[8,16]{1,0:T(8,128)(2,1)S(1)} %bitcast.5, f32[8,128,128]{2,1,0:T(8,128)S(1)} %copy-done.1, s32[8,128,128]{2,1,0:T(8,128)S(1)} %copy-done.2, s32[8,4]{1,0:T(8,128)S(1)} %copy.6.neighbour_table), custom_call_target="tpu_custom_call" | custom-call | tf_op jit(solution)/shard_map/pallas_call | solution.py:496
  83.9 0.8 copy.8
Async XLA Ops:
  0.0 0.7 copy-start.4
  0.7 0.7 copy-start.3
  1.4 1.0 %copy-start = (bf16[1,8,2,128,128]{4,3,2,1,0:T(8,128)(2,1)S(1)}, bf16[1,8,2,128,128]{4,3,2,1,0:T(8,128)(2,1)}, u32[]{:S(2)}) copy-start(bf16[1,8,2,128,128]{4,3,2,1,0:T(8,128)(2,1)} %param.5) | copy-start | bytes 1572868
  2.4 1.0 %copy-start.1 = (f32[8,128,128]{2,1,0:T(8,128)S(1)}, f32[8,128,128]{2,1,0:T(8,128)}, u32[]{:S(2)}) copy-start(f32[8,128,128]{2,1,0:T(8,128)} %diffusivity.1) | copy-start | bytes 1572868
  3.4 1.0 %copy-start.2 = (s32[8,128,128]{2,1,0:T(8,128)S(1)}, s32[8,128,128]{2,1,0:T(8,128)}, u32[]{:S(2)}) copy-start(s32[8,128,128]{2,1,0:T(8,128)} %land_mask.1) | copy-start | bytes 1572868

commit v4 on v3

--- a/solution.py
+++ b/solution.py
@@ -19,7 +19,7 @@
 SUMMED = UNITS - RAW
 TRAVEL = UNITS + RAW
 RING = 8
-LAGS = (4, 7, 9, 10)
+LAGS = (2, 4, 6, 8)
 Y_LAG = 6
 LAST = LAGS[3]
 STEPS = max(TRAVEL + LAST, SUMMED + LAST + Y_LAG)
@@ -328,7 +328,7 @@
     def sweep(source, target, c, with_strips, part=None):
         here, there = source.at[c], target.at[c]
 
-        @pl.loop(0, SLOTS, unroll=2)
+        @pl.loop(0, SLOTS, unroll=4)
         def _(t):
             results = []
             for r, size, south, north in pieces(t, with_strips, part):

time: 85 us -> 84 us (0.988); the launches traced: 84.7 us -> 82.7 us
  Pallas kernels: 79.4 us -> 77.4 us
    pallas_call x1, Pallas kernels: 79.4 us -> 77.4 us  [shards(): pl.pallas_call(kernel, out_shape=jax.ShapeDtypeStruct((SLOTS, TRACERS, N,...]
where the time goes in v4:
time: 84 us; the launch traced here: 82.7 us
  Pallas kernels  77.4 us (92%)
  local copies, waits for them, and re-layouts  5.28 us (6%)
    pallas_call x1, Pallas kernels, shards(): pl.pallas_call(kernel, out_shape=jax.ShapeDtypeStruct((SLOTS, TRACERS, N,...  77.4 us
    unnamed x12, local copies, waits for them, and re-layouts  5.28 us

profile of v4, /device:TPU:6, one launch (start us, length us, event | category | flops | bytes accessed | tf_op | source)
XLA Modules:
  0.0 82.7 jit_solution(13377829245605280715)
XLA Ops:
  0.0 0.0 copy-start.4
  0.0 0.7 copy-done.4
  0.7 0.0 copy-start.3
  0.7 0.1 copy.6.neighbour_table
  0.8 0.6 copy-done.3
  1.4 0.0 copy-start
  1.4 1.0 %copy-done = bf16[1,8,2,128,128]{4,3,2,1,0:T(8,128)(2,1)S(1)} copy-done((bf16[1,8,2,128,128]{4,3,2,1,0:T(8,128)(2,1)S(1)}, bf16[1,8,2,128,128]{4,3,2,1,0:T(8,128)(2,1)}, u32[]{:S(2)}) %copy-start) | copy-done | bytes 524312
  2.4 0.0 copy-start.1
  2.4 1.0 %copy-done.1 = f32[8,128,128]{2,1,0:T(8,128)S(1)} copy-done((f32[8,128,128]{2,1,0:T(8,128)S(1)}, f32[8,128,128]{2,1,0:T(8,128)}, u32[]{:S(2)}) %copy-start.1) | copy-done | bytes 524312
  3.4 0.0 copy-start.2
  3.5 1.0 %copy-done.2 = s32[8,128,128]{2,1,0:T(8,128)S(1)} copy-done((s32[8,128,128]{2,1,0:T(8,128)S(1)}, s32[8,128,128]{2,1,0:T(8,128)}, u32[]{:S(2)}) %copy-start.2) | copy-done | bytes 524312
  4.5 77.4 %shard_map.55 = bf16[8,2,128,128]{3,2,1,0:T(8,128)(2,1)S(1)} custom-call(bf16[8,2,128,128]{3,2,1,0:T(8,128)(2,1)S(1)} %bitcast.4, bf16[8,16]{1,0:T(8,128)(2,1)S(1)} %bitcast.5, f32[8,128,128]{2,1,0:T(8,128)S(1)} %copy-done.1, s32[8,128,128]{2,1,0:T(8,128)S(1)} %copy-done.2, s32[8,4]{1,0:T(8,128)S(1)} %copy.6.neighbour_table), custom_call_target="tpu_custom_call" | custom-call | tf_op jit(solution)/shard_map/pallas_call | solution.py:496
  81.9 0.8 copy.8
Async XLA Ops:
  0.0 0.7 copy-start.4
  0.7 0.7 copy-start.3
  1.4 1.0 %copy-start = (bf16[1,8,2,128,128]{4,3,2,1,0:T(8,128)(2,1)S(1)}, bf16[1,8,2,128,128]{4,3,2,1,0:T(8,128)(2,1)}, u32[]{:S(2)}) copy-start(bf16[1,8,2,128,128]{4,3,2,1,0:T(8,128)(2,1)} %param.5) | copy-start | bytes 1572868
  2.4 1.0 %copy-start.1 = (f32[8,128,128]{2,1,0:T(8,128)S(1)}, f32[8,128,128]{2,1,0:T(8,128)}, u32[]{:S(2)}) copy-start(f32[8,128,128]{2,1,0:T(8,128)} %diffusivity.1) | copy-start | bytes 1572868
  3.4 1.0 %copy-start.2 = (s32[8,128,128]{2,1,0:T(8,128)S(1)}, s32[8,128,128]{2,1,0:T(8,128)}, u32[]{:S(2)}) copy-start(s32[8,128,128]{2,1,0:T(8,128)} %land_mask.1) | copy-start | bytes 1572868
